TPU v7x, 32 devices: a whole 2x2x4 slice. The times are simulated.
32 devices in a mesh: dp: 16 (over z, y, core), seq: 2 (over x).
Axes of the slice: x: 2, y: 2, z: 4, core: 2. Of those that a mesh axis runs over, the one named last changes fastest.
Arguments:
- inputs: bfloat16 [16, 1024, 768], P('dp', 'seq'), may hold values from -6 to 6
- vectors: bfloat16 [768, 8], P('dp'), may hold values from -2 to 2, as said below
- w_qkv: bfloat16 [768, 2304], P('dp', 'seq'), may hold values from -0.21875 to 0.21875
- w_out: bfloat16 [768, 768], P('dp', 'seq'), may hold values from -1.25 to 1.25
- w_up: bfloat16 [768, 3072], P('dp', 'seq'), may hold values from -0.21875 to 0.21875
- w_down: bfloat16 [768, 3072], P('dp', 'seq'), may hold values from -0.109375 to 0.109375
- up_bias: bfloat16 [3072], P(('dp', 'seq')), may hold values from -3 to 3
- cotangent: bfloat16 [16, 1024, 768], P('dp', 'seq'), may hold values from -6 to 6
Outputs:
- result: bfloat16 [16, 1024, 768], P('dp', 'seq')
- input_grad: float32 [16, 1024, 768], P('dp', 'seq')
- grad_qkv: float32 [768, 2304], P('dp', 'seq')
- grad_out: float32 [768, 768], P('dp', 'seq')
- grad_up: float32 [768, 3072], P('dp', 'seq')
- grad_down: float32 [768, 3072], P('dp', 'seq')
- grad_up_bias: float32 [3072], P(('dp', 'seq'))
- grad_vectors: float32 [768, 8], P('dp')
Inputs may be any that keep to these rules, and one draw needn't show every extreme that they name: `vectors`: columns 0 and 5 are the two norms' scales, between 0.5 and 1.5; the other columns are shifts and biases.
All inputs are finite; a program needn't handle non-finite values.
Results may differ from a plain program's by a relative error of at most 0.018.
Values may be sent and summed in bfloat16 or wider, within the bound.
No kernel may reach another device: no remote copies, remote signals or barrier semaphores. Data moves between devices by JAX's collectives and lax.ppermute only.
A program may use at most 192 MiB of HBM per device.

v0:
```python
import math

import jax
import jax.numpy as jnp
from jax import lax
from jax.sharding import PartitionSpec as P

HEADS = 12
HEAD_DIM = 64


EPSILON = 1e-05
MASKED = -1e30


def norm_rows(values, scale_row, shift_row):
    row_mean = jnp.mean(values, axis=-1, keepdims=True)
    centered = values - row_mean
    variance = jnp.mean(centered * centered, axis=-1, keepdims=True)
    return centered * lax.rsqrt(variance + EPSILON) * scale_row + shift_row


def gelu_tanh(values):
    return (
        0.5
        * values
        * (1.0 + jnp.tanh(0.7978845608028654 * (values + 0.044715 * values * values * values)))
    )


def contract_last(left_side, right_side):
    return lax.dot_general(
        left_side, right_side, (((1,), (1,)), ((), ())), preferred_element_type=jnp.float32
    )


def contract_first(left_side, right_side):
    return lax.dot_general(
        left_side, right_side, (((0,), (0,)), ((), ())), preferred_element_type=jnp.float32
    )


def on_device(inputs, vectors, w_qkv, w_out, w_up, w_down, up_bias, cotangent):
    seq_count, piece_len, model_width = inputs.shape
    row_count = seq_count * piece_len
    score_scale = HEAD_DIM ** (-0.5)
    seq_index = lax.axis_index("seq")
    query_pos = seq_index * piece_len + jnp.arange(piece_len)
    qkv_cols, out_cols, up_cols, down_cols, upb_cols = (
        lax.all_gather(w_qkv, "seq", axis=1, tiled=True),
        lax.all_gather(w_out, "seq", axis=1, tiled=True),
        lax.all_gather(w_up, "seq", axis=1, tiled=True),
        lax.all_gather(w_down, "seq", axis=1, tiled=True),
        lax.all_gather(up_bias, "seq", axis=0, tiled=True),
    )
    full_fwd = (
        lax.all_gather(qkv_cols, "dp", axis=0, tiled=True),
        lax.all_gather(out_cols, "dp", axis=0, tiled=True),
        lax.all_gather(up_cols, "dp", axis=0, tiled=True),
        lax.all_gather(down_cols, "dp", axis=0, tiled=True),
        lax.all_gather(upb_cols, "dp", axis=0, tiled=True),
        lax.all_gather(vectors, "dp", axis=0, tiled=True),
    )
    qkv_full, out_full, up_full, down_full, upb_full, vec_full = full_fwd
    vec_values = vec_full.astype(jnp.float32)
    resid_in = inputs.reshape(row_count, model_width).astype(jnp.float32)
    normed_one = norm_rows(resid_in, vec_values[:, 0], vec_values[:, 1]).astype(jnp.bfloat16)
    qkv_bias = jnp.concatenate(
        [vec_values[:, 2], jnp.zeros_like(vec_values[:, 2]), vec_values[:, 3]]
    )
    qkv_rows = (
        jnp.dot(normed_one, qkv_full, preferred_element_type=jnp.float32) + qkv_bias
    ).astype(jnp.bfloat16)
    queries = qkv_rows[:, :model_width].reshape(seq_count, piece_len, HEADS, HEAD_DIM)
    key_vals = qkv_rows[:, model_width:].reshape(seq_count, piece_len, 2 * model_width)

    def block_scores(key_block, first_row):
        key_rows = key_block.shape[1]
        keys_part = key_block[..., :model_width].reshape(seq_count, key_rows, HEADS, HEAD_DIM)
        scores = (
            jnp.einsum("bqhd,bkhd->bhqk", queries, keys_part, preferred_element_type=jnp.float32)
            * score_scale
        )
        causal = (first_row + jnp.arange(key_rows))[None, :] <= query_pos[:, None]
        return jnp.where(causal, scores, MASKED)

    key_block = lax.all_gather(key_vals, "seq", axis=1, tiled=True)
    run_max = jnp.full((seq_count, HEADS, piece_len), MASKED, jnp.float32)
    key_rows = key_block.shape[1]
    values_part = key_block[..., model_width:].reshape(seq_count, key_rows, HEADS, HEAD_DIM)
    scores = block_scores(key_block, jnp.int32(0))
    new_max = jnp.maximum(run_max, jnp.max(scores, axis=-1))
    exp_scores = jnp.exp(scores - new_max[..., None])
    run_total = jnp.sum(exp_scores, axis=-1)
    added_part = jnp.einsum(
        "bhqk,bkhd->bqhd",
        exp_scores.astype(jnp.bfloat16),
        values_part,
        preferred_element_type=jnp.float32,
    )
    run_acc = added_part
    run_max, run_total, run_acc = (new_max, run_total, run_acc)
    attended = run_acc / jnp.transpose(run_total, (0, 2, 1))[..., None]
    log_total = run_max + jnp.log(run_total)
    attended_lo = attended.reshape(row_count, model_width).astype(jnp.bfloat16)
    branch_attn = (
        jnp.dot(attended_lo, out_full, preferred_element_type=jnp.float32) + vec_values[:, 4]
    )
    middle = resid_in + branch_attn
    normed_two = norm_rows(middle, vec_values[:, 5], vec_values[:, 6]).astype(jnp.bfloat16)
    up_act = jnp.dot(normed_two, up_full, preferred_element_type=jnp.float32) + upb_full.astype(
        jnp.float32
    )
    hidden = gelu_tanh(up_act).astype(jnp.bfloat16)
    branch_mlp = contract_last(hidden, down_full) + vec_values[:, 7]
    result = middle + branch_mlp
    qkv_back, out_back, up_back, down_back = (qkv_full, out_full, up_full, down_full)
    out_grad = cotangent.reshape(row_count, model_width).astype(jnp.float32)
    mlp_grad = out_grad.astype(jnp.bfloat16)
    hidden_grad = jnp.dot(mlp_grad, down_back, preferred_element_type=jnp.float32)
    gelu_pull = jax.vjp(gelu_tanh, up_act)[1]
    up_grad = gelu_pull(hidden_grad)[0].astype(jnp.bfloat16)
    norm_two_grad = contract_last(up_grad, up_back)
    ln_two_pull = jax.vjp(norm_rows, middle, vec_values[:, 5], vec_values[:, 6])[1]
    middle_part, scale_two, shift_two = ln_two_pull(norm_two_grad)
    middle_grad = out_grad + middle_part
    attn_out_grad = middle_grad.astype(jnp.bfloat16)
    attended_grad = contract_last(attn_out_grad, out_back).astype(jnp.bfloat16)
    grad_heads = attended_grad.reshape(seq_count, piece_len, HEADS, HEAD_DIM)
    row_delta = jnp.transpose(
        jnp.sum(grad_heads.astype(jnp.float32) * attended, axis=-1), (0, 2, 1)
    )
    key_vals_all = lax.all_gather(key_vals, "seq", axis=1, tiled=True)
    total_len = key_vals_all.shape[1]
    key_block_len = math.gcd(total_len, 512)

    def back_step(query_acc, block_index):
        first_row = block_index * key_block_len
        key_block = lax.dynamic_slice_in_dim(key_vals_all, first_row, key_block_len, 1)
        keys_part = key_block[..., :model_width].reshape(seq_count, key_block_len, HEADS, HEAD_DIM)
        values_part = key_block[..., model_width:].reshape(
            seq_count, key_block_len, HEADS, HEAD_DIM
        )
        scores = block_scores(key_block, first_row)
        attn_probs = jnp.exp(scores - log_total[..., None])
        prob_grad = jnp.einsum(
            "bqhd,bkhd->bhqk", grad_heads, values_part, preferred_element_type=jnp.float32
        )
        score_grad = (attn_probs * (prob_grad - row_delta[..., None])).astype(jnp.bfloat16)
        step_part = jnp.einsum(
            "bhqk,bkhd->bqhd", score_grad, keys_part, preferred_element_type=jnp.float32
        )
        key_grad = (
            jnp.einsum("bhqk,bqhd->bkhd", score_grad, queries, preferred_element_type=jnp.float32)
            * score_scale
        )
        value_grad = jnp.einsum(
            "bhqk,bqhd->bkhd",
            attn_probs.astype(jnp.bfloat16),
            grad_heads,
            preferred_element_type=jnp.float32,
        )
        key_value = jnp.concatenate(
            [
                key_grad.reshape(seq_count, key_block_len, model_width),
                value_grad.reshape(seq_count, key_block_len, model_width),
            ],
            axis=-1,
        )
        return (query_acc + step_part * score_scale, key_value)

    query_grad, kv_blocks = lax.scan(
        back_step,
        jnp.zeros((seq_count, piece_len, HEADS, HEAD_DIM), jnp.float32),
        jnp.arange(total_len // key_block_len),
    )
    kv_terms = jnp.moveaxis(kv_blocks, 0, 1).reshape(seq_count, total_len, 2 * model_width)
    key_val_grad = lax.psum_scatter(
        kv_terms.astype(jnp.bfloat16), "seq", scatter_dimension=1, tiled=True
    ).astype(jnp.float32)
    key_val_grad = key_val_grad.reshape(row_count, 2 * model_width)
    qkv_grad = jnp.concatenate(
        [query_grad.reshape(row_count, model_width), key_val_grad], axis=1
    ).astype(jnp.bfloat16)
    norm_one_grad = contract_last(qkv_grad, qkv_back)
    ln_one_pull = jax.vjp(norm_rows, resid_in, vec_values[:, 0], vec_values[:, 1])[1]
    input_part, scale_one, shift_one = ln_one_pull(norm_one_grad)
    input_grad = middle_grad + input_part
    whole_qkv = contract_first(normed_one, qkv_grad)
    whole_out = contract_first(attended_lo, attn_out_grad)
    whole_up = contract_first(normed_two, up_grad)
    whole_down = contract_first(mlp_grad, hidden)
    row_qkv, row_out, row_up, row_down = (
        lax.psum_scatter(
            whole_qkv.astype(jnp.bfloat16), "dp", scatter_dimension=0, tiled=True
        ).astype(jnp.float32),
        lax.psum_scatter(
            whole_out.astype(jnp.bfloat16), "dp", scatter_dimension=0, tiled=True
        ).astype(jnp.float32),
        lax.psum_scatter(
            whole_up.astype(jnp.bfloat16), "dp", scatter_dimension=0, tiled=True
        ).astype(jnp.float32),
        lax.psum_scatter(
            whole_down.astype(jnp.bfloat16), "dp", scatter_dimension=0, tiled=True
        ).astype(jnp.float32),
    )
    grad_qkv, grad_out, grad_up, grad_down = (
        lax.psum_scatter(
            row_qkv.astype(jnp.bfloat16), "seq", scatter_dimension=1, tiled=True
        ).astype(jnp.float32),
        lax.psum_scatter(
            row_out.astype(jnp.bfloat16), "seq", scatter_dimension=1, tiled=True
        ).astype(jnp.float32),
        lax.psum_scatter(
            row_up.astype(jnp.bfloat16), "seq", scatter_dimension=1, tiled=True
        ).astype(jnp.float32),
        lax.psum_scatter(
            row_down.astype(jnp.bfloat16), "seq", scatter_dimension=1, tiled=True
        ).astype(jnp.float32),
    )
    vec_term = jnp.stack(
        [
            scale_one,
            shift_one,
            jnp.sum(qkv_grad[:, :model_width].astype(jnp.float32), axis=0),
            jnp.sum(qkv_grad[:, 2 * model_width :].astype(jnp.float32), axis=0),
            jnp.sum(attn_out_grad.astype(jnp.float32), axis=0),
            scale_two,
            shift_two,
            jnp.sum(mlp_grad.astype(jnp.float32), axis=0),
        ],
        axis=1,
    )
    upb_term = jnp.sum(up_grad.astype(jnp.float32), axis=0)
    vec_sum, upb_sum = lax.psum((vec_term, upb_term), ("dp", "seq"))
    vec_rows = vectors.shape[0]
    grad_vectors = lax.dynamic_slice_in_dim(vec_sum, lax.axis_index("dp") * vec_rows, vec_rows, 0)
    upb_rows = up_bias.shape[0]
    upb_start = (lax.axis_index("dp") * lax.axis_size("seq") + seq_index) * upb_rows
    grad_up_bias = lax.dynamic_slice_in_dim(upb_sum, upb_start, upb_rows, 0)
    return (
        result.reshape(seq_count, piece_len, model_width).astype(jnp.bfloat16),
        input_grad.reshape(seq_count, piece_len, model_width),
        grad_qkv,
        grad_out,
        grad_up,
        grad_down,
        grad_up_bias,
        grad_vectors,
    )


def solution(mesh):
    placed = (
        P("dp", "seq", None),
        P("dp", None),
        P("dp", "seq"),
        P("dp", "seq"),
        P("dp", "seq"),
        P("dp", "seq"),
        P(("dp", "seq")),
        P("dp", "seq", None),
    )
    return jax.shard_map(
        on_device,
        mesh=mesh,
        in_specs=placed,
        out_specs=(
            P("dp", "seq", None),
            P("dp", "seq", None),
            P("dp", "seq"),
            P("dp", "seq"),
            P("dp", "seq"),
            P("dp", "seq"),
            P(("dp", "seq")),
            P("dp", None),
        ),
        check_vma=False,
    )
```

profile of v0, /device:TPU:0, one launch (start us, length us, event | category | flops | bytes accessed | tf_op | source)
XLA Modules:
  0.0 713.2 jit_solution(7653742742374191039)
XLA Ops:
  7.2 8.6 %all_gather.38 = bf16[48,2304]{1,0:T(8,128)(2,1)} all-gather(bf16[48,1152]{1,0:T(8,128)(2,1)} %param.12), channel_id=1, replica_groups=mesh['dp'=16,'seq'=2] {'seq'}, dimensions={1}, use_global_device_ids=true | all-gather | bytes 331776 | tf_op jit(solution)/shard_map/all_gather | solution.py:50
  15.9 22.2 %all-gather.1 = bf16[16,48,8]{1,2,0:T(8,128)(2,1)S(1)} all-gather(bf16[1,48,8]{1,2,0:T(8,128)(2,1)} %bitcast.234), channel_id=1, replica_groups=mesh['dp'=16,'seq'=2] {'dp'}, dimensions={0}, use_global_device_ids=true | all-gather | bytes 13056 | tf_op jit(solution)/shard_map/all_gather | solution.py:62
  42.3 21.0 %all-gather.8.cloned.1.call-done = bf16[768,2304]{1,0:T(8,128)(2,1)} async-done(((bf16[48,2304]{1,0:T(8,128)(2,1)}), bf16[768,2304]{1,0:T(8,128)(2,1)}) %all-gather.8.cloned.1.call-update) | async-done | bytes 3538960 | tf_op jit(solution)/shard_map/all_gather | solution.py:57
  75.2 8.3 %all_gather.43 = bf16[48,3072]{1,0:T(8,128)(2,1)} all-gather(bf16[48,1536]{1,0:T(8,128)(2,1)S(1)} %copy-done.21), channel_id=1, replica_groups=mesh['dp'=16,'seq'=2] {'seq'}, dimensions={1}, use_global_device_ids=true | all-gather | bytes 442368 | tf_op jit(solution)/shard_map/all_gather | solution.py:52
  83.6 9.6 %all_gather.47 = bf16[48,3072]{1,0:T(8,128)(2,1)} all-gather(bf16[48,1536]{1,0:T(8,128)(2,1)S(1)} %copy-done.22), channel_id=1, replica_groups=mesh['dp'=16,'seq'=2] {'seq'}, dimensions={1}, use_global_device_ids=true | all-gather | bytes 442368 | tf_op jit(solution)/shard_map/all_gather | solution.py:53
  101.2 30.1 %all-reduce.1 = bf16[3072]{0:T(1024)(128)(2,1)S(1)} all-reduce(bf16[3072]{0:T(1024)(128)(2,1)S(1)} %dynamic-update-slice.1), channel_id=1, replica_groups=mesh['dp'=16,'seq'=2] {'dp'}, use_global_device_ids=true, to_apply=%add.1 | all-reduce | flops 3072 | bytes 12288
  140.8 14.4 %fusion.16 = (f32[12,512]{1,0:T(8,128)S(1)}, f32[12,512,1024]{2,1,0:T(8,128)}) fusion(pred[512,1024]{1,0:T(8,128)(4,1)S(1)} %iota_compare_fusion, bf16[512,12,64]{0,2,1:T(8,128)(2,1)} %bitcast.4, bf16[1024,12,64]{0,2,1:T(8,128)(2,1)} %bitcast.216), kind=kOutput, calls=%fused_computation.27 | convolution fusion | flops 824174592 | bytes 28073984 | tf_op jit(solution)/shard_map/bqhd,bkhd->bhqk/dot_general | solution.py:81
  155.2 11.9 %fusion.17 = f32[12,512]{1,0:T(8,128)S(1)} fusion(f32[12,512,1024]{2,1,0:T(8,128)} %get-tuple-element.223, f32[12,512]{1,0:T(8,128)S(1)} %broadcast_maximum_fusion, pred[512,1024]{1,0:T(8,128)(4,1)S(1)} %iota_compare_fusion), kind=kLoop, calls=%fused_computation.28 | loop fusion | flops 25159680 | bytes 25739264 | tf_op jit(solution)/shard_map/reduce_sum | solution.py:94
  167.1 12.3 %fusion.67 = (bf16[1,512,12,64]{1,3,2,0:T(8,128)(2,1)}, f32[1,512,12,64]{1,3,2,0:T(8,128)}) fusion(f32[512,12]{0,1:T(8,128)S(1)} %bitcast.228, bf16[1024,12,64]{0,2,1:T(8,128)(2,1)S(1)} %bitcast.222, f32[12,512,1024]{2,1,0:T(8,128)} %get-tuple-element.223, f32[12,512]{1,0:T(8,128)S(1)} %broadcast_maximum_fusion, pred[512,1024]{1,0:T(8,128)(4,1)S(1)} %iota_compare_fusion), kind=kOutput, calls=%fused_computation.123 | convolution fusion | flops 831258624 | bytes 29671424 | tf_op jit(solution)/shard_map/bhqk,bkhd->bqhd/dot_general | solution.py:95
  182.3 30.4 %all-gather.12.cloned.1.call-done = bf16[768,3072]{1,0:T(8,128)(2,1)} async-done(((bf16[48,3072]{1,0:T(8,128)(2,1)}), bf16[768,3072]{1,0:T(8,128)(2,1)}) %all-gather.12.cloned.1.call-update) | async-done | bytes 4718608 | tf_op jit(solution)/shard_map/all_gather | solution.py:59
  219.8 47.0 %all-gather.14.cloned.1.call-done = bf16[768,3072]{1,0:T(8,128)(2,1)} async-done(((bf16[48,3072]{1,0:T(8,128)(2,1)}), bf16[768,3072]{1,0:T(8,128)(2,1)}) %all-gather.14.cloned.1.call-update) | async-done | bytes 4718608 | tf_op jit(solution)/shard_map/all_gather | solution.py:60
  266.8 11.7 %convert_reduce_fusion = (f32[3072]{0:T(1024)}, bf16[512,3072]{1,0:T(8,128)(2,1)S(1)}) fusion(bf16[768,3072]{1,0:T(8,128)(2,1)} %all-gather.14.cloned.1.call-done, bf16[1,512,768]{2,1,0:T(8,128)(2,1)S(1)} %copy-done.13, f32[512,3072]{1,0:T(8,128)} %fusion.62, f32[3072]{0:T(1024)S(1)} %convert_element_type.145), kind=kOutput, calls=%fused_computation.42 | convolution fusion | flops 2458383360 | bytes 14966784 | tf_op jit(solution)/shard_map/dot_general | solution.py:120
  290.5 76.7 %while.13 = (s32[]{:T(128)}, f32[1,512,12,64]{1,3,2,0:T(8,128)}, bf16[2,1,512,1536]{3,2,0,1:T(8,128)(2,1)}, s32[2]{0:T(128)S(1)}, bf16[1,1024,1536]{2,1,0:T(8,12...) while((s32[]{:T(128)}, f32[1,512,12,64]{1,3,2,0:T(8,128)}, ...), condition=%wide.region_10.11_spmd.clone, body=%wide.region_9.10_spmd.clone.sunk | while | flops 2050098176 | bytes 121192840 | solution.py:172
  302.1 9.0 %fusion.115 = bf16[12,512,512]{1,2,0:T(8,128)(2,1)} fusion(f32[12,512,512]{2,1,0:T(8,128)} %fusion.114, f32[12,512]{1,0:T(8,128)S(1)} %bitcast.231, f32[12,512]{1,0:T(8,128)S(1)} %bitcast.232, pred[512,512]{0,1:T(8,128)(4,1)S(1)} %broadcast_compare_fusion.2, bf16[512,12,64]{0,2,1:T(8,128)(2,1)S(1)} %bitcast.213, bf16[1,512,12,64]{1,3,2,0:T(8,128)(2,1)} %copy-done.11), kind=kOutput, calls=%fused_computation.2.clone.1 | convolution fusion | flops 421527552 | bytes 20758528 | tf_op jit(solution)/shard_map/while/body/eval_jaxpr/bqhd,bkhd->bhqk/dot_general | solution.py:146
  315.2 8.4 %fusion.116 = bf16[12,512,64]{1,2,0:T(8,128)(2,1)S(1)} fusion(f32[12,512,512]{2,1,0:T(8,128)} %fusion.114, f32[12,512]{1,0:T(8,128)S(1)} %bitcast.233, pred[512,512]{0,1:T(8,128)(4,1)S(1)} %broadcast_compare_fusion.2, bf16[1,512,12,64]{1,3,2,0:T(8,128)(2,1)} %copy-done.11), kind=kOutput, calls=%fused_computation.7.clone.1 | convolution fusion | flops 415236096 | bytes 14442496 | tf_op jit(solution)/shard_map/while/body/eval_jaxpr/bhqk,bqhd->bkhd/dot_general | solution.py:157
  340.3 8.9 %fusion.115 = bf16[12,512,512]{1,2,0:T(8,128)(2,1)} fusion(f32[12,512,512]{2,1,0:T(8,128)} %fusion.114, f32[12,512]{1,0:T(8,128)S(1)} %bitcast.231, f32[12,512]{1,0:T(8,128)S(1)} %bitcast.232, pred[512,512]{0,1:T(8,128)(4,1)S(1)} %broadcast_compare_fusion.2, bf16[512,12,64]{0,2,1:T(8,128)(2,1)S(1)} %bitcast.213, bf16[1,512,12,64]{1,3,2,0:T(8,128)(2,1)} %copy-done.11), kind=kOutput, calls=%fused_computation.2.clone.1 | convolution fusion | flops 421527552 | bytes 20758528 | tf_op jit(solution)/shard_map/while/body/eval_jaxpr/bqhd,bkhd->bhqk/dot_general | solution.py:146
  353.4 8.4 %fusion.116 = bf16[12,512,64]{1,2,0:T(8,128)(2,1)S(1)} fusion(f32[12,512,512]{2,1,0:T(8,128)} %fusion.114, f32[12,512]{1,0:T(8,128)S(1)} %bitcast.233, pred[512,512]{0,1:T(8,128)(4,1)S(1)} %broadcast_compare_fusion.2, bf16[1,512,12,64]{1,3,2,0:T(8,128)(2,1)} %copy-done.11), kind=kOutput, calls=%fused_computation.7.clone.1 | convolution fusion | flops 415236096 | bytes 14442496 | tf_op jit(solution)/shard_map/while/body/eval_jaxpr/bhqk,bqhd->bkhd/dot_general | solution.py:157
  376.8 8.7 %fusion.28 = bf16[768,3072]{0,1:T(8,128)(2,1)} fusion(bf16[1,512,768]{2,1,0:T(8,128)(2,1)S(1)} %copy-done.14, f32[512,3072]{1,0:T(8,128)} %fusion.62, f32[3072]{0:T(1024)S(1)} %convert_element_type.145), kind=kOutput, calls=%fused_computation.48 | convolution fusion | flops 2434007040 | bytes 11808768 | tf_op jit(solution)/shard_map/dot_general | solution.py:38
  394.1 15.3 %reduce-scatter.16.cloned.1.call-done = bf16[1,512,1536]{2,1,0:T(8,128)(2,1)} async-done(((bf16[1,1024,1536]{2,1,0:T(8,128)(2,1)}), bf16[1,512,1536]{2,1,0:T(8,128)(2,1)}) %reduce-scatter.16.cloned.1.call-update) | async-done | bytes 1572880 | tf_op jit(solution)/shard_map/reduce_scatter | solution.py:178
  416.3 9.2 %fusion.46 = bf16[1,512,768]{2,1,0:T(8,128)(2,1)} fusion(f32[512,768]{1,0:T(8,128)S(1)} %copy-done.9, bf16[768,3072]{1,0:T(8,128)(2,1)} %all-gather.14.cloned.1.call-done, f32[768]{0:T(1024)S(1)} %copy-done.36, f32[512,3072]{1,0:T(8,128)} %fusion.62, f32[3072]{0:T(1024)S(1)} %convert_element_type.145), kind=kOutput, calls=%fused_computation.85 | convolution fusion | flops 2432827392 | bytes 13384704 | tf_op jit(solution)/shard_map/dot_general | solution.py:32
  427.1 76.2 %reduce-scatter.22.cloned.1.call-done = bf16[48,3072]{1,0:T(8,128)(2,1)} async-done(((bf16[768,3072]{1,0:T(8,128)(2,1)}), bf16[48,3072]{1,0:T(8,128)(2,1)}) %reduce-scatter.22.cloned.1.call-update) | async-done | bytes 294928 | tf_op jit(solution)/shard_map/reduce_scatter | solution.py:200
  509.3 72.3 %reduce-scatter.32.cloned.1.call-done = bf16[48,3072]{1,0:T(8,128)(2,1)} async-done(((bf16[768,3072]{1,0:T(8,128)(2,1)}), bf16[48,3072]{1,0:T(8,128)(2,1)}) %reduce-scatter.32.cloned.1.call-update) | async-done | bytes 294928
  587.5 65.5 %reduce-scatter.18.cloned.1.call-done = bf16[48,2304]{1,0:T(8,128)(2,1)} async-done(((bf16[768,2304]{1,0:T(8,128)(2,1)}), bf16[48,2304]{1,0:T(8,128)(2,1)}) %reduce-scatter.18.cloned.1.call-update) | async-done | bytes 221200 | tf_op jit(solution)/shard_map/reduce_scatter | solution.py:194
  658.5 40.2 %all-reduce.2 = (f32[3072]{0:T(1024)S(1)}, f32[768,8]{0,1:T(8,128)S(1)}) all-reduce(f32[3072]{0:T(1024)S(1)} %copy-done.35, f32[768,8]{0,1:T(8,128)S(1)} %stack.35), channel_id=1, replica_groups=mesh['dp'=16,'seq'=2] {'dp','seq'}, use_global_device_ids=true, to_apply=%region_23.24 | all-reduce | flops 9216 | bytes 73728 | tf_op jit(solution)/shard_map/psum | solution.py:235
  (253 shorter events, 145.4 us)
Async XLA Ops:
  7.2 56.1 %copy-start.5 = (bf16[1,512,768]{2,1,0:T(8,128)(2,1)S(1)}, bf16[1,512,768]{2,1,0:T(8,128)(2,1)}, u32[]{:S(2)}) copy-start(bf16[1,512,768]{2,1,0:T(8,128)(2,1)} %param.10) | copy-start | bytes 2359300
  7.2 56.1 %all-gather.8.cloned.1.call-start = ((), (), s32[]{:S(2)}) async-start(), calls=%async_computation.9 | async-start | bytes 3760128 | tf_op jit(solution)/shard_map/all_gather | solution.py:57
  15.9 117.0 %all-gather.16.cloned.1.call-start = ((), (), s32[]{:S(2)}) async-start(), calls=%async_computation.19 | async-start | bytes 4718592 | tf_op jit(solution)/shard_map/all_gather | solution.py:87
  38.9 28.6 %copy-start.37 = (f32[768]{0:T(1024)}, f32[768]{0:T(1024)S(1)}, u32[]{:S(2)}) copy-start(f32[768]{0:T(1024)S(1)} %get-tuple-element.184) | copy-start | bytes 9220
  38.9 173.8 %copy-start.39 = (f32[768]{0:T(1024)}, f32[768]{0:T(1024)S(1)}, u32[]{:S(2)}) copy-start(f32[768]{0:T(1024)S(1)} %get-tuple-element.180) | copy-start | bytes 9220
  70.2 61.5 %slice-start.2 = ((bf16[512,2304]{1,0:T(8,128)(2,1)}), bf16[512,768]{1,0:T(8,128)(2,1)S(1)}, s32[]{:S(2)}) async-start(bf16[512,2304]{1,0:T(8,128)(2,1)} %copy-done.10), calls=%async_computation.25 | async-start | bytes 1572864 | tf_op jit(solution)/shard_map/slice | solution.py:74
  70.2 109.3 %all-gather.10.cloned.1.call-start = ((), (), s32[]{:S(2)}) async-start(), calls=%async_computation.10 | async-start | bytes 1253376 | tf_op jit(solution)/shard_map/all_gather | solution.py:58
  75.1 137.5 %all-gather.12.cloned.1.call-start = ((), (), s32[]{:S(2)}) async-start(), calls=%async_computation.11 | async-start | bytes 5013504 | tf_op jit(solution)/shard_map/all_gather | solution.py:59
  83.5 183.3 %all-gather.14.cloned.1.call-start = ((), (), s32[]{:S(2)}) async-start(), calls=%async_computation.12 | async-start | bytes 5013504 | tf_op jit(solution)/shard_map/all_gather | solution.py:60
  93.2 274.1 %reduce-scatter.20.cloned.1.call-start = ((), (), s32[]{:S(2)}) async-start(), calls=%async_computation.15 | async-start | bytes 1253376 | tf_op jit(solution)/shard_map/reduce_scatter | solution.py:197
  181.9 100.1 %copy-start.7 = (f32[512,768]{1,0:T(8,128)}, f32[512,768]{1,0:T(8,128)S(1)}, u32[]{:S(2)}) copy-start(f32[512,768]{1,0:T(8,128)S(1)} %get-tuple-element.227) | copy-start | bytes 4718596
  212.7 54.1 %copy-start.13 = (bf16[1,512,768]{2,1,0:T(8,128)(2,1)S(1)}, bf16[1,512,768]{2,1,0:T(8,128)(2,1)}, u32[]{:S(2)}) copy-start(bf16[1,512,768]{2,1,0:T(8,128)(2,1)} %param.17) | copy-start | bytes 2359300
  290.2 119.3 %reduce-scatter.16.cloned.1.call-start = ((), (), s32[]{:S(2)}) async-start(), calls=%async_computation.13 | async-start | bytes 4718592 | tf_op jit(solution)/shard_map/reduce_scatter | solution.py:178
  367.2 58.2 %reduce-scatter.30.cloned.1.call-start = ((), (), s32[]{:S(2)}) async-start(), calls=%async_computation.21 | async-start | bytes 294912
  369.1 134.1 %reduce-scatter.22.cloned.1.call-start = ((), (), s32[]{:S(2)}) async-start(), calls=%async_computation.16 | async-start | bytes 5013504 | tf_op jit(solution)/shard_map/reduce_scatter | solution.py:200
  375.7 205.9 %reduce-scatter.32.cloned.1.call-start = ((), (), s32[]{:S(2)}) async-start(), calls=%async_computation.22 | async-start | bytes 5013504
  392.2 260.8 %reduce-scatter.18.cloned.1.call-start = ((), (), s32[]{:S(2)}) async-start(), calls=%async_computation.14 | async-start | bytes 3760128 | tf_op jit(solution)/shard_map/reduce_scatter | solution.py:194
  414.9 285.0 %reduce-scatter.24.cloned.1.call-start = ((), (), s32[]{:S(2)}) async-start(), calls=%async_computation.17 | async-start | bytes 442368 | tf_op jit(solution)/shard_map/reduce_scatter | solution.py:214
  416.3 87.3 %copy-start.19 = (bf16[512,768]{1,0:T(8,128)(2,1)S(1)}, bf16[512,768]{1,0:T(8,128)(2,1)}, u32[]{:S(2)}) copy-start(bf16[512,768]{1,0:T(8,128)(2,1)} %copy-done.18) | copy-start | bytes 2359300
  503.3 198.3 %reduce-scatter.26.cloned.1.call-start = ((), (), s32[]{:S(2)}) async-start(), calls=%async_computation.18 | async-start | bytes 1179648 | tf_op jit(solution)/shard_map/reduce_scatter | solution.py:217
  583.8 71.3 %copy-start.4 = (f32[512,768]{1,0:T(8,128)S(1)}, f32[512,768]{1,0:T(8,128)}, u32[]{:S(2)}) copy-start(f32[512,768]{1,0:T(8,128)} %copy-done.3) | copy-start | bytes 4718596
  583.8 71.3 %copy-start.15 = (bf16[1,512,768]{2,1,0:T(8,128)(2,1)S(1)}, bf16[1,512,768]{2,1,0:T(8,128)(2,1)}, u32[]{:S(2)}) copy-start(bf16[1,512,768]{2,1,0:T(8,128)(2,1)} %param.17) | copy-start | bytes 2359300
  583.8 71.3 %copy-start.33 = (f32[512]{0:T(512)S(1)}, f32[512]{0:T(512)}, u32[]{:S(2)}) copy-start(f32[512]{0:T(512)} %copy-done.32) | copy-start | bytes 6148
  583.8 120.5 %reduce-scatter.28.cloned.1.call-start = ((), (), s32[]{:S(2)}) async-start(), calls=%async_computation.20 | async-start | bytes 884736
  (48 other events, 422.7 us)
Sparse Core Ops, SparseCore 0:
  16.0 47.2 all-gather.7
  70.3 47.8 all-gather.15
  120.5 37.6 all-gather.9
  160.3 52.3 all-gather.11
  214.8 51.9 all-gather.13
  290.3 56.6 reduce-scatter.19
  367.4 42.0 reduce-scatter.15
  412.3 10.9 reduce-scatter.29
  427.7 75.5 reduce-scatter.21
  506.9 74.6 reduce-scatter.31
  586.0 67.0 reduce-scatter.17
  655.2 11.0 reduce-scatter.23
  668.7 17.7 reduce-scatter.25
  688.6 15.7 reduce-scatter.27
where the time goes:
time: 719 us; the launch traced here: 713 us
  waiting for transfers between devices  329 us (46%)
  matrix products  160 us (22%)
  blocking collectives  129 us (18%)
  local copies, waits for them, and re-layouts  48.6 us (7%)
  other arithmetic  28 us (4%)
  between operations  16.3 us (2%)
    reduce_scatter x1, waiting for transfers between devices, on_device(): lax.psum_scatter(whole_up.astype(jnp.bfloat16), 'dp', scatter_dimension=0...  76.2 us
    unnamed x17, waiting for transfers between devices  73.4 us
    reduce_scatter x1, waiting for transfers between devices, on_device(): lax.psum_scatter(whole_qkv.astype(jnp.bfloat16), 'dp', scatter_dimension=...  65.5 us
    all_gather x1, waiting for transfers between devices, on_device(): lax.all_gather(down_cols, 'dp', axis=0, tiled=True)  47 us
    psum x1, blocking collectives, on_device(): vec_sum, upb_sum = lax.psum((vec_term, upb_term), ('dp', 'seq'))  40.2 us
    unnamed x2, blocking collectives  35 us
    all_gather x1, waiting for transfers between devices, on_device(): lax.all_gather(up_cols, 'dp', axis=0, tiled=True)  30.4 us
    dot_general x3, matrix products, block_scores(): jnp.einsum('bqhd,bkhd->bhqk', queries, keys_part, preferred_element_type=...  29.5 us
  transfers between devices with their start and end apart: 14, of which 8 were waited for; matrix products, arithmetic and copies ran while one was open for 28% of the time, Pallas kernels for 0%

commit v1 on v0

--- a/solution.py
+++ b/solution.py
@@ -1,12 +1,16 @@
+import functools
 import math
 
 import jax
 import jax.numpy as jnp
 from jax import lax
+from jax.experimental import pallas as pl
+from jax.experimental.pallas import tpu as pltpu
 from jax.sharding import PartitionSpec as P
 
 HEADS = 12
 HEAD_DIM = 64
+VMEM_LIMIT = 48 * 1024 * 1024
 
 
 EPSILON = 1e-05
@@ -40,7 +44,7 @@
     )
 
 
-def on_device(inputs, vectors, w_qkv, w_out, w_up, w_down, up_bias, cotangent):
+def on_device_general(inputs, vectors, w_qkv, w_out, w_up, w_down, up_bias, cotangent):
     seq_count, piece_len, model_width = inputs.shape
     row_count = seq_count * piece_len
     score_scale = HEAD_DIM ** (-0.5)
@@ -250,6 +254,471 @@
     )
 
 
+def bit_masks(count):
+    return [1 << k for k in range(count.bit_length() - 1)]
+
+
+def hops(n_dp, n_seq, seq_first):
+    dp_bits = bit_masks(n_dp)
+    far = [("dp", mask) for mask in reversed(dp_bits[2:])]
+    middle = [("dp", mask) for mask in dp_bits[1:2]]
+    across = [("seq", mask) for mask in reversed(bit_masks(n_seq))]
+    near = [("dp", mask) for mask in dp_bits[:1]]
+    return far + (across + middle if seq_first else middle + across) + near
+
+
+def exchange(values, hop, sizes):
+    axis, mask = hop
+    return lax.ppermute(values, axis, [(i, i ^ mask) for i in range(sizes[axis])])
+
+
+def slot_owner(slot, path):
+    offset = {"dp": 0, "seq": 0}
+    for k, (axis, mask) in enumerate(path):
+        if slot >> k & 1:
+            offset[axis] ^= mask
+    return offset["dp"], offset["seq"]
+
+
+def gather_slots(block, path, sizes):
+    held = block[None]
+    for hop in path[:-1]:
+        held = jnp.concatenate([held, exchange(held, hop, sizes)], axis=0)
+    return held, exchange(held, path[-1], sizes)
+
+
+def place_kernel(path, rows, first, cols, stride, me_ref, held_ref, other_ref, out_ref, sem):
+    half = 1 << (len(path) - 1)
+    copies = []
+    for slot in range(2 * half):
+        off_dp, off_seq = slot_owner(slot, path)
+        row = pl.multiple_of((me_ref[0] ^ off_dp) * rows, 16)
+        col = pl.multiple_of((me_ref[1] ^ off_seq) * stride, 128)
+        src = (held_ref if slot < half else other_ref).at[slot % half, :, pl.ds(first, cols)]
+        dst = out_ref.at[pl.ds(row, rows), pl.ds(col, cols)]
+        copies.append(pltpu.make_async_copy(src, dst, sem.at[slot]))
+    for copy in copies:
+        copy.start()
+    for copy in copies:
+        copy.wait()
+
+
+def place(held, other, path, sizes, pair, first, cols):
+    half, rows, _ = held.shape
+    whole_seq = any(axis == "seq" for axis, _ in path)
+    shape = (rows * sizes["dp"], cols * (sizes["seq"] if whole_seq else 1))
+    return pl.pallas_call(
+        functools.partial(place_kernel, path, rows, first, cols, cols if whole_seq else 0),
+        out_shape=jax.ShapeDtypeStruct(shape, held.dtype),
+        in_specs=[pl.BlockSpec(memory_space=pltpu.SMEM)] + [pl.BlockSpec(memory_space=pl.ANY)] * 2,
+        out_specs=pl.BlockSpec(memory_space=pltpu.VMEM),
+        scratch_shapes=[pltpu.SemaphoreType.DMA((2 * half,))],
+        compiler_params=pltpu.CompilerParams(vmem_limit_bytes=VMEM_LIMIT),
+        cost_estimate=pl.CostEstimate(
+            flops=0, bytes_accessed=4 * shape[0] * shape[1], transcendentals=0
+        ),
+    )(pair, held, other)
+
+
+def split_kernel(path, rows, widths, strides, me_ref, *refs):
+    wholes, keep_ref, send_ref, sem = refs[: len(widths)], refs[-3], refs[-2], refs[-1]
+    half = 1 << (len(path) - 1)
+    copies = []
+    for slot in range(2 * half):
+        off_dp, off_seq = slot_owner(slot, path)
+        row = pl.multiple_of((me_ref[0] ^ off_dp) * rows, 16)
+        at = 0
+        for k, (whole_ref, width) in enumerate(zip(wholes, widths)):
+            col = pl.multiple_of((me_ref[1] ^ off_seq) * strides[k], 128)
+            src = whole_ref.at[pl.ds(row, rows), pl.ds(col, width)]
+            target = keep_ref if slot < half else send_ref
+            dst = target.at[slot % half, :, pl.ds(at, width)]
+            copies.append(pltpu.make_async_copy(src, dst, sem.at[slot, k]))
+            at += width
+    for copy in copies:
+        copy.start()
+    for copy in copies:
+        copy.wait()
+
+
+def split(wholes, path, sizes, pair):
+    whole_seq = any(axis == "seq" for axis, _ in path)
+    rows = wholes[0].shape[0] // sizes["dp"]
+    widths = [whole.shape[1] // (sizes["seq"] if whole_seq else 1) for whole in wholes]
+    half = 1 << (len(path) - 1)
+    shape = jax.ShapeDtypeStruct((half, rows, sum(widths)), wholes[0].dtype)
+    size = 2 * half * rows * sum(widths)
+    return pl.pallas_call(
+        functools.partial(
+            split_kernel, path, rows, widths, widths if whole_seq else [0] * len(widths)
+        ),
+        out_shape=[shape, shape],
+        in_specs=[pl.BlockSpec(memory_space=pltpu.SMEM)]
+        + [pl.BlockSpec(memory_space=pltpu.VMEM)] * len(wholes),
+        out_specs=[pl.BlockSpec(memory_space=pl.ANY)] * 2,
+        scratch_shapes=[pltpu.SemaphoreType.DMA((2 * half, len(wholes)))],
+        compiler_params=pltpu.CompilerParams(vmem_limit_bytes=VMEM_LIMIT),
+        cost_estimate=pl.CostEstimate(flops=0, bytes_accessed=4 * size, transcendentals=0),
+    )(pair, *wholes)
+
+
+def reduce_slots(keep, send, path, sizes):
+    for hop in reversed(path):
+        other = exchange(send, hop, sizes)
+        half = keep.shape[0] // 2
+        if half == 0:
+            return keep[0].astype(jnp.float32) + other[0].astype(jnp.float32)
+        send = (keep[half:].astype(jnp.float32) + other[half:].astype(jnp.float32)).astype(
+            jnp.bfloat16
+        )
+        keep = (keep[:half].astype(jnp.float32) + other[:half].astype(jnp.float32)).astype(
+            jnp.bfloat16
+        )
+
+
+def head_lanes(values, head, width):
+    lane = lax.broadcasted_iota(jnp.int32, values.shape, 1)
+    return jnp.where(lane // width == head, values, jnp.zeros_like(values))
+
+
+def later_keys(block):
+    key_at = lax.broadcasted_iota(jnp.int32, (block, block), 0)
+    query_at = lax.broadcasted_iota(jnp.int32, (block, block), 1)
+    return key_at > query_at
+
+
+def scores_of(keys, query, hidden_keys, block):
+    scores = contract_last(keys, query)
+    last = jnp.where(hidden_keys, MASKED, scores[-block:])
+    if scores.shape[0] == block:
+        return last
+    return jnp.concatenate([scores[:-block], last], axis=0)
+
+
+def attend_kernel(block, width, q_ref, k_ref, v_ref, out_ref, lse_ref):
+    length, lanes = q_ref.shape
+    scale = jnp.bfloat16(width ** (-0.5))
+    hidden_keys = later_keys(block)
+    values_t = v_ref[...].T
+    for first in range(0, length, block):
+        last = first + block
+        queries = q_ref[first:last, :] * scale
+        outs = []
+        for head in range(lanes // width):
+            scores = scores_of(k_ref[:last, :], head_lanes(queries, head, width), hidden_keys, block)
+            top = jnp.max(scores, axis=0, keepdims=True)
+            probs = jnp.exp(scores - top)
+            total = jnp.sum(probs, axis=0, keepdims=True)
+            mixed = jnp.dot(
+                values_t[head * width : (head + 1) * width, :last],
+                probs.astype(jnp.bfloat16),
+                preferred_element_type=jnp.float32,
+            )
+            outs.append(mixed / total)
+            lse_ref[head : head + 1, first:last] = top + jnp.log(total)
+        out_ref[first:last, :] = jnp.concatenate(outs, axis=0).T.astype(jnp.bfloat16)
+
+
+def attend_back_kernel(
+    block, width, q_ref, k_ref, v_ref, g_ref, o_ref, lse_ref, dq_ref, dk_ref, dv_ref, dk_acc, dv_acc
+):
+    length, lanes = q_ref.shape
+    heads = lanes // width
+    scale = jnp.bfloat16(width ** (-0.5))
+    hidden_keys = later_keys(block)
+    keys_t = k_ref[...].T
+    for first in reversed(range(0, length, block)):
+        last = first + block
+        queries = q_ref[first:last, :] * scale
+        grads = g_ref[first:last, :]
+        products = (grads.astype(jnp.float32) * o_ref[first:last, :].astype(jnp.float32)).T
+        key_part = value_part = None
+        query_parts = []
+        for head in range(heads):
+            query = head_lanes(queries, head, width)
+            grad = head_lanes(grads, head, width)
+            scores = scores_of(k_ref[:last, :], query, hidden_keys, block)
+            probs = jnp.exp(scores - lse_ref[head : head + 1, first:last])
+            delta = jnp.sum(products[head * width : (head + 1) * width], axis=0, keepdims=True)
+            prob_grad = contract_last(v_ref[:last, :], grad)
+            score_grad = (probs * (prob_grad - delta)).astype(jnp.bfloat16)
+            key_term = jnp.dot(score_grad, query, preferred_element_type=jnp.float32)
+            value_term = jnp.dot(
+                probs.astype(jnp.bfloat16), grad, preferred_element_type=jnp.float32
+            )
+            key_part = key_term if key_part is None else key_part + key_term
+            value_part = value_term if value_part is None else value_part + value_term
+            query_parts.append(
+                jnp.dot(
+                    keys_t[head * width : (head + 1) * width, :last],
+                    score_grad,
+                    preferred_element_type=jnp.float32,
+                )
+            )
+        query_grad = jnp.concatenate(query_parts, axis=0).T * width ** (-0.5)
+        dq_ref[first:last, :] = query_grad.astype(jnp.bfloat16)
+        if last == length:
+            dk_acc[...] = key_part
+            dv_acc[...] = value_part
+        else:
+            dk_acc[:last, :] += key_part
+            dv_acc[:last, :] += value_part
+    dk_ref[...] = dk_acc[...].astype(jnp.bfloat16)
+    dv_ref[...] = dv_acc[...].astype(jnp.bfloat16)
+
+
+def pair_spec(length, first):
+    return pl.BlockSpec((length, 128), lambda pair: (0, first + pair))
+
+
+def attend(qkv):
+    length, cols = qkv.shape
+    pairs = cols // 3 // 128
+    return pl.pallas_call(
+        functools.partial(attend_kernel, 256, HEAD_DIM),
+        grid=(pairs,),
+        out_shape=[
+            jax.ShapeDtypeStruct((length, cols // 3), jnp.bfloat16),
+            jax.ShapeDtypeStruct((8 * pairs, length), jnp.float32),
+        ],
+        in_specs=[pair_spec(length, k * pairs) for k in range(3)],
+        out_specs=[pair_spec(length, 0), pl.BlockSpec((8, length), lambda pair: (pair, 0))],
+        compiler_params=pltpu.CompilerParams(vmem_limit_bytes=VMEM_LIMIT),
+        cost_estimate=pl.CostEstimate(
+            flops=2 * length * length * cols // 3,
+            bytes_accessed=8 * length * cols // 3,
+            transcendentals=length * length * pairs,
+        ),
+    )(qkv, qkv, qkv)
+
+
+def attend_back(qkv, grads, attended, lse):
+    length, cols = qkv.shape
+    pairs = cols // 3 // 128
+    shape = jax.ShapeDtypeStruct((length, cols // 3), jnp.bfloat16)
+    return pl.pallas_call(
+        functools.partial(attend_back_kernel, 256, HEAD_DIM),
+        grid=(pairs,),
+        out_shape=[shape] * 3,
+        in_specs=[pair_spec(length, k * pairs) for k in range(3)]
+        + [pair_spec(length, 0)] * 2
+        + [pl.BlockSpec((8, length), lambda pair: (pair, 0))],
+        out_specs=[pair_spec(length, 0)] * 3,
+        scratch_shapes=[pltpu.VMEM((length, 128), jnp.float32)] * 2,
+        compiler_params=pltpu.CompilerParams(vmem_limit_bytes=VMEM_LIMIT),
+        cost_estimate=pl.CostEstimate(
+            flops=5 * length * length * cols // 3,
+            bytes_accessed=16 * length * cols // 3,
+            transcendentals=length * length * pairs,
+        ),
+    )(qkv, qkv, qkv, grads, attended, lse)
+
+
+def in_order(seq_index, mine, other, axis):
+    return jnp.where(
+        seq_index == 0,
+        jnp.concatenate([mine, other], axis=axis),
+        jnp.concatenate([other, mine], axis=axis),
+    )
+
+
+def on_device(inputs, vectors, w_qkv, w_out, w_up, w_down, up_bias, cotangent):
+    _, piece_len, model_width = inputs.shape
+    sizes = {"dp": lax.axis_size("dp"), "seq": lax.axis_size("seq")}
+    seq_index = lax.axis_index("seq")
+    pair = jnp.stack([lax.axis_index("dp"), seq_index])
+    swap = ("seq", 1)
+    half_width = model_width // 2
+    path_dp = [hop for hop in hops(sizes["dp"], sizes["seq"], True) if hop[0] == "dp"]
+    path_a = hops(sizes["dp"], sizes["seq"], True)
+    path_b = hops(sizes["dp"], sizes["seq"], False)
+    rows = w_qkv.shape[0]
+    per_row = up_bias.shape[0] // rows
+
+    bias_cols = up_bias.reshape(per_row, rows).T
+    small_own = jnp.concatenate(
+        [vectors, bias_cols, jnp.zeros((rows, 128 - 8 - per_row), vectors.dtype)], axis=1
+    )
+    blocks = [w_qkv[:, k * half_width : (k + 1) * half_width] for k in range(3)]
+    arrived = exchange(jnp.concatenate([blocks[1], small_own], axis=1), swap, sizes)
+    head_cols = jnp.where(
+        seq_index == 0,
+        jnp.concatenate([blocks[0], blocks[2], arrived[:, :half_width]], axis=1),
+        jnp.concatenate([arrived[:, :half_width], blocks[0], blocks[2]], axis=1),
+    )
+    bias_other = arrived[:, half_width + 8 : half_width + 8 + per_row]
+    small_cols = jnp.concatenate(
+        [
+            vectors,
+            in_order(seq_index, bias_cols, bias_other, 1),
+            jnp.zeros((rows, 128 - 8 - 2 * per_row), vectors.dtype),
+        ],
+        axis=1,
+    )
+    first_held, first_other = gather_slots(
+        jnp.concatenate([head_cols, small_cols], axis=1), path_dp, sizes
+    )
+    x_own = inputs.reshape(piece_len, model_width)
+    x_all = in_order(seq_index, x_own, exchange(x_own, swap, sizes), 0).astype(jnp.float32)
+    a_held, a_other = gather_slots(jnp.concatenate([w_out, w_up], axis=1), path_a, sizes)
+    b_held, b_other = gather_slots(w_down, path_b, sizes)
+
+    first_whole = place(first_held, first_other, path_dp, sizes, pair, 0, 3 * half_width + 128)
+    qkv_full = first_whole[:, : 3 * half_width]
+    small = first_whole[:, 3 * half_width :].astype(jnp.float32)
+    vec_values = small[:, :8]
+    upb_full = jnp.transpose(
+        small[:, 8 : 8 + 2 * per_row].reshape(sizes["dp"], rows, 2 * per_row), (0, 2, 1)
+    ).reshape(-1)
+
+    def own_heads(vector):
+        return lax.dynamic_slice_in_dim(vector, seq_index * half_width, half_width, 0)
+
+    qkv_bias = jnp.concatenate(
+        [
+            own_heads(vec_values[:, 2]),
+            jnp.zeros((half_width,), jnp.float32),
+            own_heads(vec_values[:, 3]),
+        ]
+    )
+    normed_one = norm_rows(x_all, vec_values[:, 0], vec_values[:, 1]).astype(jnp.bfloat16)
+    qkv_rows = (
+        jnp.dot(normed_one, qkv_full, preferred_element_type=jnp.float32) + qkv_bias
+    ).astype(jnp.bfloat16)
+    attended, lse = attend(qkv_rows)
+
+    def tokens_of(values, index):
+        return lax.dynamic_slice_in_dim(values, index * piece_len, piece_len, 0)
+
+    attended_lo = in_order(
+        seq_index,
+        tokens_of(attended, seq_index),
+        exchange(tokens_of(attended, 1 - seq_index), swap, sizes),
+        1,
+    )
+    resid_in = x_own.astype(jnp.float32)
+    out_full = place(a_held, a_other, path_a, sizes, pair, 0, w_out.shape[1])
+    up_full = place(a_held, a_other, path_a, sizes, pair, w_out.shape[1], w_up.shape[1])
+    down_full = place(b_held, b_other, path_b, sizes, pair, 0, w_down.shape[1])
+    branch_attn = (
+        jnp.dot(attended_lo, out_full, preferred_element_type=jnp.float32) + vec_values[:, 4]
+    )
+    middle = resid_in + branch_attn
+    normed_two = norm_rows(middle, vec_values[:, 5], vec_values[:, 6]).astype(jnp.bfloat16)
+    up_act = jnp.dot(normed_two, up_full, preferred_element_type=jnp.float32) + upb_full
+    hidden = gelu_tanh(up_act).astype(jnp.bfloat16)
+    mlp_grad = cotangent.reshape(piece_len, model_width)
+    out_grad = mlp_grad.astype(jnp.float32)
+
+    def reduce(wholes, path):
+        keep, send = split([whole.astype(jnp.bfloat16) for whole in wholes], path, sizes, pair)
+        return reduce_slots(keep, send, path, sizes)
+
+    grad_down = reduce([contract_first(mlp_grad, hidden)], path_a)
+    branch_mlp = contract_last(hidden, down_full) + vec_values[:, 7]
+    result = middle + branch_mlp
+    hidden_grad = jnp.dot(mlp_grad, down_full, preferred_element_type=jnp.float32)
+    gelu_pull = jax.vjp(gelu_tanh, up_act)[1]
+    up_grad = gelu_pull(hidden_grad)[0].astype(jnp.bfloat16)
+    whole_up = contract_first(normed_two, up_grad)
+    norm_two_grad = contract_last(up_grad, up_full)
+    ln_two_pull = jax.vjp(norm_rows, middle, vec_values[:, 5], vec_values[:, 6])[1]
+    middle_part, scale_two, shift_two = ln_two_pull(norm_two_grad)
+    middle_grad = out_grad + middle_part
+    attn_out_grad = middle_grad.astype(jnp.bfloat16)
+    attended_grad = contract_last(attn_out_grad, out_full).astype(jnp.bfloat16)
+
+    def heads_of(values, index):
+        return lax.dynamic_slice_in_dim(values, index * half_width, half_width, 1)
+
+    grad_heads = in_order(
+        seq_index,
+        heads_of(attended_grad, seq_index),
+        exchange(heads_of(attended_grad, 1 - seq_index), swap, sizes),
+        0,
+    )
+    grad_up_out = reduce([whole_up, contract_first(attended_lo, attn_out_grad)], path_b)
+    grad_up, grad_out = (
+        grad_up_out[:, : w_up.shape[1]],
+        grad_up_out[:, w_up.shape[1] :],
+    )
+    query_grad, key_grad, value_grad = attend_back(qkv_rows, grad_heads, attended, lse)
+    qkv_grad = jnp.concatenate([query_grad, key_grad, value_grad], axis=1)
+    norm_one_grad = contract_last(qkv_grad, qkv_full)
+    norm_one_own = tokens_of(norm_one_grad, seq_index) + exchange(
+        tokens_of(norm_one_grad, 1 - seq_index).astype(jnp.bfloat16), swap, sizes
+    ).astype(jnp.float32)
+    ln_one_pull = jax.vjp(norm_rows, resid_in, vec_values[:, 0], vec_values[:, 1])[1]
+    input_part, _, _ = ln_one_pull(norm_one_own)
+    input_grad = middle_grad + input_part
+
+    centered = x_all - jnp.mean(x_all, axis=-1, keepdims=True)
+    variance = jnp.mean(centered * centered, axis=-1, keepdims=True)
+    scale_one = jnp.sum(norm_one_grad * (centered * lax.rsqrt(variance + EPSILON)), axis=0)
+    shift_one = jnp.sum(norm_one_grad, axis=0)
+
+    def of_own_heads(sums):
+        none = jnp.zeros_like(sums)
+        return jnp.where(
+            seq_index == 0, jnp.concatenate([sums, none]), jnp.concatenate([none, sums])
+        )
+
+    vec_term = jnp.stack(
+        [
+            scale_one,
+            shift_one,
+            of_own_heads(jnp.sum(query_grad.astype(jnp.float32), axis=0)),
+            of_own_heads(jnp.sum(value_grad.astype(jnp.float32), axis=0)),
+            jnp.sum(attn_out_grad.astype(jnp.float32), axis=0),
+            scale_two,
+            shift_two,
+            jnp.sum(mlp_grad.astype(jnp.float32), axis=0),
+        ],
+        axis=1,
+    )
+    upb_term = jnp.sum(up_grad.astype(jnp.float32), axis=0)
+    upb_cols = jnp.transpose(
+        upb_term.reshape(sizes["dp"], 2 * per_row, rows), (0, 2, 1)
+    ).reshape(model_width, 2 * per_row)
+    small_grads = jnp.concatenate(
+        [vec_term, upb_cols, jnp.zeros((model_width, 128 - 8 - 2 * per_row), jnp.float32)], axis=1
+    )
+    last = reduce([contract_first(normed_one, qkv_grad), small_grads], path_dp)
+    small_last = last[:, 3 * half_width :]
+    sent = jnp.where(
+        seq_index == 0, last[:, 2 * half_width :],
+        jnp.concatenate([last[:, :half_width], small_last], axis=1)
+    )
+    arrived_last = exchange(sent.astype(jnp.bfloat16), swap, sizes).astype(jnp.float32)
+    middle_block = arrived_last[:, :half_width]
+    kept = jnp.where(seq_index == 0, last[:, : 2 * half_width], last[:, half_width : 3 * half_width])
+    grad_qkv = jnp.concatenate([kept[:, :half_width], middle_block, kept[:, half_width:]], axis=1)
+    small_sum = small_last + arrived_last[:, half_width:]
+    grad_vectors = small_sum[:, :8]
+    bias_own = lax.dynamic_slice_in_dim(small_sum, 8 + seq_index * per_row, per_row, 1)
+    grad_up_bias = bias_own.T.reshape(-1)
+    return (
+        result.reshape(1, piece_len, model_width).astype(jnp.bfloat16),
+        input_grad.reshape(1, piece_len, model_width),
+        grad_qkv,
+        grad_out,
+        grad_up,
+        grad_down,
+        grad_up_bias,
+        grad_vectors,
+    )
+
+
+def block(*arrays):
+    n_dp, n_seq = lax.axis_size("dp"), lax.axis_size("seq")
+    rows = arrays[2].shape[0]
+    whole_tiles = rows % 16 == 0 and all(weight.shape[1] % 384 == 0 for weight in arrays[2:6])
+    powers = n_dp >= 4 and n_dp & (n_dp - 1) == 0
+    if n_seq == 2 and powers and whole_tiles and arrays[0].shape[0] == 1:
+        return on_device(*arrays)
+    return on_device_general(*arrays)
+
+
 def solution(mesh):
     placed = (
         P("dp", "seq", None),
@@ -262,7 +731,7 @@
         P("dp", "seq", None),
     )
     return jax.shard_map(
-        on_device,
+        block,
         mesh=mesh,
         in_specs=placed,
         out_specs=(

time: 719 us -> 372 us (0.52)
  waiting for transfers between devices: 329 us -> 173 us
  blocking collectives: 129 us -> 0 us
  matrix products: 160 us -> 49.6 us
  Pallas kernels: 0 us -> 53.2 us
  starting transfers between devices: 1.12 us -> 35.6 us
  between operations: 16.3 us -> 1.71 us
  local copies, waits for them, and re-layouts: 48.6 us -> 34.8 us
  other arithmetic: 28 us -> 19.4 us
    ppermute x0 -> x34, waiting for transfers between devices: none -> 173 us  [exchange(): lax.ppermute(values, axis, [(i, i ^ mask) for i in range(sizes[axis])])]
    reduce_scatter x6 -> x0, waiting for transfers between devices: 157 us -> none  [the longest x1 76.2 us: on_device(): lax.psum_scatter(whole_up.astype(jnp.bfloat16), 'dp', scatter_dimension=0...]
    all_gather x5 -> x0, waiting for transfers between devices: 98.4 us -> none  [the longest x1 47 us: on_device(): lax.all_gather(down_cols, 'dp', axis=0, tiled=True)]
    dot_general x14 -> x2, matrix products: 110 us -> 12.6 us  [the longest x1 7.77 us: on_device(): jnp.dot(mlp_grad, down_full, preferred_element_type=jnp.float32)]
    unnamed x17 -> x0, waiting for transfers between devices: 73.4 us -> none
    all_gather x5 -> x0, blocking collectives: 53.6 us -> none  [the longest x1 22.2 us: on_device(): lax.all_gather(vectors, 'dp', axis=0, tiled=True)]
    pallas_call x0 -> x9, Pallas kernels: none -> 53.2 us  [the longest x4 16.6 us: place(): pl.pallas_call(functools.partial(place_kernel, path, rows, first, cols, c...]
    psum x1 -> x0, blocking collectives: 40.2 us -> none  [on_device(): vec_sum, upb_sum = lax.psum((vec_term, upb_term), ('dp', 'seq'))]
  transfers between devices with their start and end apart: 14 -> 34, of which waited for: 8 -> 16; matrix products, arithmetic and copies ran while one was open for 28% -> 19% of each run, Pallas kernels for 0% -> 13%
where the time goes in v1:
time: 372 us; the launch traced here: 367 us
  waiting for transfers between devices  173 us (47%)
  Pallas kernels  53.2 us (14%)
  matrix products  49.6 us (13%)
  starting transfers between devices  35.6 us (10%)
  local copies, waits for them, and re-layouts  34.8 us (9%)
  other arithmetic  19.4 us (5%)
    ppermute x34, waiting for transfers between devices, exchange(): lax.ppermute(values, axis, [(i, i ^ mask) for i in range(sizes[axis])])  173 us
    ppermute x34, starting transfers between devices, exchange(): lax.ppermute(values, axis, [(i, i ^ mask) for i in range(sizes[axis])])  35.6 us
    dot_general x4, matrix products, contract_first(): lax.dot_general(left_side, right_side, (((0,), (0,)), ((), ())), preferre...  19.5 us
    pallas_call x4, Pallas kernels, place(): pl.pallas_call(functools.partial(place_kernel, path, rows, first, cols, c...  16.6 us
    pallas_call x1, Pallas kernels, attend_back(): pl.pallas_call(functools.partial(attend_back_kernel, 256, HEAD_DIM), grid...  13.5 us
    pallas_call x1, Pallas kernels, attend(): pl.pallas_call(functools.partial(attend_kernel, 256, HEAD_DIM), grid=(pai...  12.4 us
    dot_general x4, matrix products, contract_last(): lax.dot_general(left_side, right_side, (((1,), (1,)), ((), ())), preferre...  11.3 us
    unnamed x71, local copies, waits for them, and re-layouts  10.7 us
  transfers between devices with their start and end apart: 34, of which 16 were waited for; matrix products, arithmetic and copies ran while one was open for 19% of the time, Pallas kernels for 13%

profile of v1, /device:TPU:0, one launch (start us, length us, event | category | flops | bytes accessed | tf_op | source)
XLA Modules:
  0.0 367.4 jit_solution(5442587259463831200)
XLA Ops:
  13.7 8.8 %collective-permute-done.7 = bf16[1,48,1920]{2,1,0:T(8,128)(2,1)S(1)} collective-permute-done((bf16[1,48,1920]{2,1,0:T(8,128)(2,1)S(1)}, bf16[1,48,1920]{2,1,0:T(8,128)(2,1)S(1)}, u32[]{:S(2)}, u32[]{:S(2)}) %collective-permute-start.7) | collective-permute-done | bytes 184352 | tf_op jit(solution)/shard_map/ppermute | solution.py:272
  26.1 10.7 %collective-permute-done.8 = bf16[2,48,1920]{2,1,0:T(8,128)(2,1)S(1)} collective-permute-done((bf16[2,48,1920]{2,1,0:T(8,128)(2,1)S(1)}, bf16[2,48,1920]{2,1,0:T(8,128)(2,1)S(1)}, u32[]{:S(2)}, u32[]{:S(2)}) %collective-permute-start.8) | collective-permute-done | bytes 368672 | tf_op jit(solution)/shard_map/ppermute | solution.py:272
  39.1 7.5 %collective-permute-done.3 = bf16[2,48,1280]{2,1,0:T(8,128)(2,1)S(1)} collective-permute-done((bf16[2,48,1280]{2,1,0:T(8,128)(2,1)S(1)}, bf16[2,48,1280]{2,1,0:T(8,128)(2,1)S(1)}, u32[]{:S(2)}, u32[]{:S(2)}) %collective-permute-start.3) | collective-permute-done | bytes 245792 | tf_op jit(solution)/shard_map/ppermute | solution.py:272
  56.4 46.1 %collective-permute-done.14 = bf16[4,48,1536]{2,1,0:T(8,128)(2,1)S(1)} collective-permute-done((bf16[4,48,1536]{2,1,0:T(8,128)(2,1)S(1)}, bf16[4,48,1536]{2,1,0:T(8,128)(2,1)S(1)}, u32[]{:S(2)}, u32[]{:S(2)}) %collective-permute-start.14) | collective-permute-done | bytes 589856 | tf_op jit(solution)/shard_map/ppermute | solution.py:272
  106.9 21.1 %collective-permute-done.15 = bf16[8,48,1536]{2,1,0:T(8,128)(2,1)S(1)} collective-permute-done((bf16[8,48,1536]{2,1,0:T(8,128)(2,1)S(1)}, bf16[8,48,1536]{2,1,0:T(8,128)(2,1)S(1)}, u32[]{:S(2)}, u32[]{:S(2)}) %collective-permute-start.15) | collective-permute-done | bytes 1179680 | tf_op jit(solution)/shard_map/ppermute | solution.py:272
  135.5 4.2 %add_convert_fusion.q_ref.k_ref.v_ref = bf16[1024,1152]{1,0:T(8,128)(2,1)S(1)} fusion(f32[1152]{0:T(1024)S(1)} %pad_maximum_fusion.10, bf16[768,1280]{1,0:T(8,128)(2,1)S(1)} %shard_map.143, f32[768]{0:T(1024)S(1)} %get-tuple-element.104, f32[768]{0:T(1024)S(1)} %get-tuple-element.103, f32[1024]{0:T(1024)S(1)} %add_rsqrt_fusion, ...), kind=kOutput, calls=%fused_computation.18 | convolution fusion | flops 1826095104 | bytes 5726209 | tf_op jit(solution)/shard_map/dot_general | solution.py:586
  139.8 12.4 %shard_map.144 = (bf16[1024,384]{1,0:T(8,128)(2,1)S(1)}, f32[24,1024]{1,0:T(8,128)S(1)}) custom-call(bf16[1024,1152]{1,0:T(8,128)(2,1)S(1)} %add_convert_fusion.q_ref.k_ref.v_ref, bf16[1024,1152]{1,0:T(8,128)(2,1)S(1)} %add_convert_fusion.q_ref.k_ref.v_ref, bf16[1024,1152]{1,0:T(8,128)(2,1)S(1)} %add_convert_fusion.q_ref.k_ref.v_ref), custom_call_target="tpu_custom_call" | custom-call | flops 805306368 | bytes 3145728 | tf_op jit(solution)/shard_map/pallas_call | solution.py:477
  154.7 5.4 %shard_map.147 = bf16[768,3072]{1,0:T(8,128)(2,1)} custom-call(s32[2]{0:T(128)S(1)} %pad_add_fusion.me_ref, bf16[16,48,1536]{2,1,0:T(8,128)(2,1)} %constant_dynamic-update-slice_fusion.5.held_ref, bf16[16,48,1536]{2,1,0:T(8,128)(2,1)} %collective-permute-done.16.other_ref), custom_call_target="tpu_custom_call" | custom-call | bytes 9437184 | tf_op jit(solution)/shard_map/pallas_call | solution.py:310
  167.4 5.5 %shard_map.146 = bf16[768,3072]{1,0:T(8,128)(2,1)} custom-call(s32[2]{0:T(128)S(1)} %pad_add_fusion.me_ref, bf16[16,48,1920]{2,1,0:T(8,128)(2,1)} %constant_dynamic-update-slice_fusion.held_ref, bf16[16,48,1920]{2,1,0:T(8,128)(2,1)} %collective-permute-done.11.other_ref), custom_call_target="tpu_custom_call" | custom-call | bytes 9437184 | tf_op jit(solution)/shard_map/pallas_call | solution.py:310
  172.8 4.9 %fusion.37 = f32[512,3072]{1,0:T(8,128)S(1)} fusion(bf16[768,3072]{1,0:T(8,128)(2,1)} %shard_map.146, f32[512,768]{1,0:T(8,128)S(1)} %get-tuple-element.117, f32[768]{0:T(1024)S(1)} %get-tuple-element.106, f32[768]{0:T(1024)S(1)} %get-tuple-element.108, f32[512]{0:T(512)S(1)} %fusion.31, f32[512]{0:T(512)S(1)} %broadcast_multiply_fusion.2), kind=kOutput, calls=%fused_computation.152 | convolution fusion | flops 2417885184 | bytes 12593152 | tf_op jit(solution)/shard_map/dot_general | solution.py:608
  177.8 7.8 %fusion.47 = (bf16[3072]{0:T(1024)(128)(2,1)S(1)}, bf16[512,3072]{1,0:T(8,128)(2,1)S(1)}) fusion(bf16[768,3072]{1,0:T(8,128)(2,1)S(1)} %bitcast.78, bf16[1,512,768]{2,1,0:T(8,128)(2,1)S(1)} %copy-done.11, f32[512,3072]{1,0:T(8,128)S(1)} %fusion.37, f32[3072]{0:T(1024)S(1)} %add.245), kind=kOutput, calls=%fused_computation.161 | convolution fusion | flops 2456810496 | bytes 14960640 | tf_op jit(solution)/shard_map/dot_general | solution.py:620
  185.6 5.0 %fusion.26 = bf16[1,512,768]{2,1,0:T(8,128)(2,1)} fusion(f32[512,768]{1,0:T(8,128)S(1)} %get-tuple-element.117, bf16[768,3072]{1,0:T(8,128)(2,1)S(1)} %bitcast.78, f32[768]{0:T(1024)S(1)} %get-tuple-element.107, f32[512,3072]{1,0:T(8,128)S(1)} %fusion.37, f32[3072]{0:T(1024)S(1)} %add.245), kind=kOutput, calls=%fused_computation.65 | convolution fusion | flops 2432827392 | bytes 13384704 | tf_op jit(solution)/shard_map/dot_general | solution.py:36
  196.8 4.8 %convolution_convert_fusion.1.refs_0_ = bf16[768,3072]{1,0:T(8,128)(2,1)} fusion(bf16[512,3072]{1,0:T(8,128)(2,1)S(1)} %get-tuple-element.121, f32[512,768]{1,0:T(8,128)S(1)} %get-tuple-element.117, f32[768]{0:T(1024)S(1)} %get-tuple-element.106, f32[768]{0:T(1024)S(1)} %get-tuple-element.108, f32[512]{0:T(512)S(1)} %fusion.31, ...), kind=kOutput, calls=%fused_computation.17 | convolution fusion | flops 2420244480 | bytes 9447424 | tf_op jit(solution)/shard_map/dot_general | solution.py:42
  207.3 5.2 %shard_map.150 = (bf16[16,48,1920]{2,1,0:T(8,128)(2,1)S(1)}, bf16[16,48,1920]{2,1,0:T(8,128)(2,1)}) custom-call(s32[2]{0:T(128)S(1)} %pad_add_fusion.me_ref, bf16[768,3072]{1,0:T(8,128)(2,1)} %convolution_convert_fusion.1.refs_0_, bf16[768,768]{1,0:T(8,128)(2,1)S(1)} %convolution_convert_fusion.3.refs_1_), custom_call_target="tpu_custom_call" | custom-call | bytes 11796480 | tf_op jit(solution)/shard_map/pallas_call | solution.py:351
  215.6 13.5 %shard_map.148 = (bf16[1024,384]{1,0:T(8,128)(2,1)S(1)}, bf16[1024,384]{1,0:T(8,128)(2,1)S(1)}, bf16[1024,384]{1,0:T(8,128)(2,1)S(1)}) custom-call(bf16[1024,1152]{1,0:T(8,128)(2,1)} %copy-done, bf16[1024,1152]{1,0:T(8,128)(2,1)} %copy-done, bf16[1024,1152]{1,0:T(8,128)(2,1)} %copy-done, bf16[1024,384]{1,0:T(8,128)(2,1)S(1)} %maximum_select_fusion.2.g_ref, ...), custom_call_target="tpu_custom_call" | custom-call | flops 2013265920 | bytes 6291456 | tf_op jit(solution)/shard_map/pallas_call | solution.py:499
  242.8 4.3 %convolution_convert_fusion.2.refs_0_ = bf16[768,1152]{1,0:T(8,128)(2,1)S(1)} fusion(bf16[1024,1152]{1,0:T(8,128)(2,1)} %copy-done.19, f32[768]{0:T(1024)} %copy-done.24, f32[768]{0:T(1024)S(1)} %get-tuple-element.103, f32[1024]{0:T(1024)} %copy-done.23, f32[1024]{0:T(1024)} %copy-done.20, bf16[512,768]{1,0:T(8,128)(2,1)S(1)} %copy-done.15, ...), kind=kOutput, calls=%fused_computation.26 | convolution fusion | flops 1824620544 | bytes 5715969 | tf_op jit(solution)/shard_map/dot_general | solution.py:42
  249.0 8.2 %fusion.9.refs_0_ = bf16[768,3072]{1,0:T(8,128)(2,1)} fusion(bf16[1,512,768]{2,1,0:T(8,128)(2,1)S(1)} %copy-done.11, f32[512,3072]{1,0:T(8,128)} %copy-done.25, f32[3072]{0:T(1024)S(1)} %copy-done.22), kind=kOutput, calls=%fused_computation.19 | convolution fusion | flops 2434007040 | bytes 11808768 | tf_op jit(solution)/shard_map/dot_general | solution.py:42
  264.9 11.0 %collective-permute-done.20 = bf16[4,48,1280]{2,1,0:T(8,128)(2,1)S(1)} collective-permute-done((bf16[4,48,1280]{2,1,0:T(8,128)(2,1)S(1)}, bf16[4,48,1280]{2,1,0:T(8,128)(2,1)S(1)}, u32[]{:S(2)}, u32[]{:S(2)}) %collective-permute-start.20) | collective-permute-done | bytes 491552 | tf_op jit(solution)/shard_map/ppermute | solution.py:272
  278.3 5.1 %collective-permute-done.21 = bf16[2,48,1280]{2,1,0:T(8,128)(2,1)S(1)} collective-permute-done((bf16[2,48,1280]{2,1,0:T(8,128)(2,1)S(1)}, bf16[2,48,1280]{2,1,0:T(8,128)(2,1)S(1)}, u32[]{:S(2)}, u32[]{:S(2)}) %collective-permute-start.21) | collective-permute-done | bytes 245792 | tf_op jit(solution)/shard_map/ppermute | solution.py:272
  283.4 4.6 %collective-permute-start.22 = (bf16[1,48,1280]{2,1,0:T(8,128)(2,1)S(1)}, bf16[1,48,1280]{2,1,0:T(8,128)(2,1)S(1)}, u32[]{:S(2)}, u32[]{:S(2)}) collective-permute-start(bf16[1,48,1280]{2,1,0:T(8,128)(2,1)S(1)} %add_convert_fusion.23), channel_id=1, source_target_pairs={{0,16},{2,18},{4,20},{6,22},{8,24},{10,26},{12,28},{14,30},{16,0},... | collective-permute-start | bytes 368648 | tf_op jit(solution)/shard_map/ppermute | solution.py:272
  295.8 30.6 %collective-permute-done.23 = bf16[48,512]{1,0:T(8,128)(2,1)S(1)} collective-permute-done((bf16[48,512]{1,0:T(8,128)(2,1)S(1)}, bf16[48,512]{1,0:T(8,128)(2,1)S(1)}, u32[]{:S(2)}, u32[]{:S(2)}) %collective-permute-start.23) | collective-permute-done | bytes 49184 | tf_op jit(solution)/shard_map/ppermute | solution.py:272
  334.3 6.1 %collective-permute-done.31 = bf16[4,48,1536]{2,1,0:T(8,128)(2,1)S(1)} collective-permute-done((bf16[4,48,1536]{2,1,0:T(8,128)(2,1)}, bf16[4,48,1536]{2,1,0:T(8,128)(2,1)S(1)}, u32[]{:S(2)}, u32[]{:S(2)}) %collective-permute-start.31) | collective-permute-done | bytes 589856 | tf_op jit(solution)/shard_map/ppermute | solution.py:272
  345.4 6.3 %collective-permute-done.32 = bf16[2,48,1536]{2,1,0:T(8,128)(2,1)S(1)} collective-permute-done((bf16[2,48,1536]{2,1,0:T(8,128)(2,1)S(1)}, bf16[2,48,1536]{2,1,0:T(8,128)(2,1)S(1)}, u32[]{:S(2)}, u32[]{:S(2)}) %collective-permute-start.32) | collective-permute-done | bytes 294944 | tf_op jit(solution)/shard_map/ppermute | solution.py:272
  351.8 4.4 %collective-permute-done.27 = bf16[2,48,1920]{2,1,0:T(8,128)(2,1)S(1)} collective-permute-done((bf16[2,48,1920]{2,1,0:T(8,128)(2,1)S(1)}, bf16[2,48,1920]{2,1,0:T(8,128)(2,1)S(1)}, u32[]{:S(2)}, u32[]{:S(2)}) %collective-permute-start.27) | collective-permute-done | bytes 368672 | tf_op jit(solution)/shard_map/ppermute | solution.py:272
  (240 shorter events, 122.4 us)
Async XLA Ops:
  7.2 15.3 %collective-permute-start.7 = (bf16[1,48,1920]{2,1,0:T(8,128)(2,1)S(1)}, bf16[1,48,1920]{2,1,0:T(8,128)(2,1)S(1)}, u32[]{:S(2)}, u32[]{:S(2)}) collective-permute-start(bf16[1,48,1920]{2,1,0:T(8,128)(2,1)S(1)} %maximum_bitcast_fusion), channel_id=1, source_target_pairs={{0,16},{2,18},{4,20},{6,22},{8,24},{10,26},{12,28},{14,30},{16,0},... | collective-permute-start | bytes 552968 | tf_op jit(solution)/shard_map/ppermute | solution.py:272
  9.8 46.1 %collective-permute-start = (bf16[512,768]{1,0:T(8,128)(2,1)}, bf16[512,768]{1,0:T(8,128)(2,1)S(1)}, u32[]{:S(2)}, u32[]{:S(2)}) collective-permute-start(bf16[512,768]{1,0:T(8,128)(2,1)} %bitcast.71), channel_id=1, source_target_pairs={{0,1},{1,0},{2,3},{3,2},{4,5},{5,4},{6,7},{7,6},{8,9},{9,8},{10,11... | collective-permute-start | bytes 2359304 | tf_op jit(solution)/shard_map/ppermute | solution.py:272
  10.4 15.6 %collective-permute-start.12 = (bf16[1,48,1536]{2,1,0:T(8,128)(2,1)}, bf16[1,48,1536]{2,1,0:T(8,128)(2,1)S(1)}, u32[]{:S(2)}, u32[]{:S(2)}) collective-permute-start(bf16[1,48,1536]{2,1,0:T(8,128)(2,1)} %bitcast.81), channel_id=1, source_target_pairs={{0,16},{2,18},{4,20},{6,22},{8,24},{10,26},{12,28},{14,30},{16,0},... | collective-permute-start | bytes 442376 | tf_op jit(solution)/shard_map/ppermute | solution.py:272
  22.6 14.2 %collective-permute-start.8 = (bf16[2,48,1920]{2,1,0:T(8,128)(2,1)S(1)}, bf16[2,48,1920]{2,1,0:T(8,128)(2,1)S(1)}, u32[]{:S(2)}, u32[]{:S(2)}) collective-permute-start(bf16[2,48,1920]{2,1,0:T(8,128)(2,1)S(1)} %pad_maximum_fusion.6), channel_id=1, source_target_pairs={{0,8},{2,10},{4,12},{6,14},{8,0},{10,2},{12,4},{14,6},{16,24},{18,... | collective-permute-start | bytes 1105928 | tf_op jit(solution)/shard_map/ppermute | solution.py:272
  22.9 14.5 %collective-permute-start.2 = (bf16[1,48,1280]{2,1,0:T(8,128)(2,1)S(1)}, bf16[1,48,1280]{2,1,0:T(8,128)(2,1)S(1)}, u32[]{:S(2)}, u32[]{:S(2)}) collective-permute-start(bf16[1,48,1280]{2,1,0:T(8,128)(2,1)S(1)} %bitcast.85), channel_id=1, source_target_pairs={{0,16},{2,18},{4,20},{6,22},{8,24},{10,26},{12,28},{14,30},{16,0},... | collective-permute-start | bytes 368648 | tf_op jit(solution)/shard_map/ppermute | solution.py:272
  26.0 27.7 %collective-permute-start.13 = (bf16[2,48,1536]{2,1,0:T(8,128)(2,1)S(1)}, bf16[2,48,1536]{2,1,0:T(8,128)(2,1)S(1)}, u32[]{:S(2)}, u32[]{:S(2)}) collective-permute-start(bf16[2,48,1536]{2,1,0:T(8,128)(2,1)S(1)} %pad_maximum_fusion.7), channel_id=1, source_target_pairs={{0,8},{2,10},{4,12},{6,14},{8,0},{10,2},{12,4},{14,6},{16,24},{18,... | collective-permute-start | bytes 884744 | tf_op jit(solution)/shard_map/ppermute | solution.py:272
  36.9 15.1 %collective-permute-start.9 = (bf16[4,48,1920]{2,1,0:T(8,128)(2,1)S(1)}, bf16[4,48,1920]{2,1,0:T(8,128)(2,1)S(1)}, u32[]{:S(2)}, u32[]{:S(2)}) collective-permute-start(bf16[4,48,1920]{2,1,0:T(8,128)(2,1)S(1)} %pad_maximum_fusion.3), channel_id=1, source_target_pairs={{0,1},{1,0},{2,3},{3,2},{4,5},{5,4},{6,7},{7,6},{8,9},{9,8},{10,11... | collective-permute-start | bytes 2211848 | tf_op jit(solution)/shard_map/ppermute | solution.py:272
  46.7 58.7 %collective-permute-start.4 = (bf16[4,48,1280]{2,1,0:T(8,128)(2,1)S(1)}, bf16[4,48,1280]{2,1,0:T(8,128)(2,1)S(1)}, u32[]{:S(2)}, u32[]{:S(2)}) collective-permute-start(bf16[4,48,1280]{2,1,0:T(8,128)(2,1)S(1)} %pad_maximum_fusion.5), channel_id=1, source_target_pairs={{0,4},{2,6},{4,0},{6,2},{8,12},{10,14},{12,8},{14,10},{16,20},{18,... | collective-permute-start | bytes 1474568 | tf_op jit(solution)/shard_map/ppermute | solution.py:272
  52.1 52.0 %collective-permute-start.10 = (bf16[8,48,1920]{2,1,0:T(8,128)(2,1)S(1)}, bf16[8,48,1920]{2,1,0:T(8,128)(2,1)S(1)}, u32[]{:S(2)}, u32[]{:S(2)}) collective-permute-start(bf16[8,48,1920]{2,1,0:T(8,128)(2,1)S(1)} %pad_maximum_fusion), channel_id=1, source_target_pairs={{0,4},{2,6},{4,0},{6,2},{8,12},{10,14},{12,8},{14,10},{16,20},{18,... | collective-permute-start | bytes 4423688 | tf_op jit(solution)/shard_map/ppermute | solution.py:272
  53.8 48.7 %collective-permute-start.14 = (bf16[4,48,1536]{2,1,0:T(8,128)(2,1)S(1)}, bf16[4,48,1536]{2,1,0:T(8,128)(2,1)S(1)}, u32[]{:S(2)}, u32[]{:S(2)}) collective-permute-start(bf16[4,48,1536]{2,1,0:T(8,128)(2,1)S(1)} %pad_maximum_fusion.4), channel_id=1, source_target_pairs={{0,4},{2,6},{4,0},{6,2},{8,12},{10,14},{12,8},{14,10},{16,20},{18,... | collective-permute-start | bytes 1769480 | tf_op jit(solution)/shard_map/ppermute | solution.py:272
  102.6 25.4 %collective-permute-start.15 = (bf16[8,48,1536]{2,1,0:T(8,128)(2,1)S(1)}, bf16[8,48,1536]{2,1,0:T(8,128)(2,1)S(1)}, u32[]{:S(2)}, u32[]{:S(2)}) collective-permute-start(bf16[8,48,1536]{2,1,0:T(8,128)(2,1)S(1)} %pad_maximum_fusion.1), channel_id=1, source_target_pairs={{0,1},{1,0},{2,3},{3,2},{4,5},{5,4},{6,7},{7,6},{8,9},{9,8},{10,11... | collective-permute-start | bytes 3538952 | tf_op jit(solution)/shard_map/ppermute | solution.py:272
  105.4 54.8 %collective-permute-start.11 = (bf16[16,48,1920]{2,1,0:T(8,128)(2,1)}, bf16[16,48,1920]{2,1,0:T(8,128)(2,1)}, u32[]{:S(2)}, u32[]{:S(2)}) collective-permute-start(bf16[16,48,1920]{2,1,0:T(8,128)(2,1)} %constant_dynamic-update-slice_fusion.held_ref), channel_id=1, source_target_pairs={{0,2},{2,0},{4,6},{6,4},{8,10},{10,8},{12,14},{14,12},{16,18},{18,... | collective-permute-start | bytes 8847368 | tf_op jit(solution)/shard_map/ppermute | solution.py:272
  105.5 24.5 %collective-permute-start.5 = (bf16[8,48,1280]{2,1,0:T(8,128)(2,1)S(1)}, bf16[8,48,1280]{2,1,0:T(8,128)(2,1)S(1)}, u32[]{:S(2)}, u32[]{:S(2)}) collective-permute-start(bf16[8,48,1280]{2,1,0:T(8,128)(2,1)S(1)} %pad_maximum_fusion.2.held_ref), channel_id=1, source_target_pairs={{0,2},{2,0},{4,6},{6,4},{8,10},{10,8},{12,14},{14,12},{16,18},{18,... | collective-permute-start | bytes 2949128 | tf_op jit(solution)/shard_map/ppermute | solution.py:272
  129.1 25.6 %collective-permute-start.16 = (bf16[16,48,1536]{2,1,0:T(8,128)(2,1)}, bf16[16,48,1536]{2,1,0:T(8,128)(2,1)}, u32[]{:S(2)}, u32[]{:S(2)}) collective-permute-start(bf16[16,48,1536]{2,1,0:T(8,128)(2,1)} %constant_dynamic-update-slice_fusion.5.held_ref), channel_id=1, source_target_pairs={{0,2},{2,0},{4,6},{6,4},{8,10},{10,8},{12,14},{14,12},{16,18},{18,... | collective-permute-start | bytes 7077896 | tf_op jit(solution)/shard_map/ppermute | solution.py:272
  196.2 17.8 %collective-permute-start.17 = (bf16[512,384]{1,0:T(8,128)(2,1)}, bf16[512,384]{1,0:T(8,128)(2,1)}, u32[]{:S(2)}, u32[]{:S(2)}) collective-permute-start(bf16[512,384]{1,0:T(8,128)(2,1)} %get-tuple-element.98), channel_id=1, source_target_pairs={{0,1},{1,0},{2,3},{3,2},{4,5},{5,4},{6,7},{7,6},{8,9},{9,8},{10,11... | collective-permute-start | bytes 1179656 | tf_op jit(solution)/shard_map/ppermute | solution.py:272
  214.1 76.3 %collective-permute-start.24 = (bf16[16,48,1920]{2,1,0:T(8,128)(2,1)}, bf16[16,48,1920]{2,1,0:T(8,128)(2,1)}, u32[]{:S(2)}, u32[]{:S(2)}) collective-permute-start(bf16[16,48,1920]{2,1,0:T(8,128)(2,1)} %get-tuple-element.27), channel_id=1, source_target_pairs={{0,2},{2,0},{4,6},{6,4},{8,10},{10,8},{12,14},{14,12},{16,18},{18,... | collective-permute-start | bytes 8847368 | tf_op jit(solution)/shard_map/ppermute | solution.py:272
  234.6 26.9 %collective-permute-start.18 = (bf16[512,768]{1,0:T(8,128)(2,1)}, bf16[512,768]{1,0:T(8,128)(2,1)S(1)}, u32[]{:S(2)}, u32[]{:S(2)}) collective-permute-start(bf16[512,768]{1,0:T(8,128)(2,1)} %dynamic-slice_convert_fusion), channel_id=1, source_target_pairs={{0,1},{1,0},{2,3},{3,2},{4,5},{5,4},{6,7},{7,6},{8,9},{9,8},{10,11... | collective-permute-start | bytes 2359304 | tf_op jit(solution)/shard_map/ppermute | solution.py:272
  248.7 13.5 %collective-permute-start.19 = (bf16[8,48,1280]{2,1,0:T(8,128)(2,1)S(1)}, bf16[8,48,1280]{2,1,0:T(8,128)(2,1)S(1)}, u32[]{:S(2)}, u32[]{:S(2)}) collective-permute-start(bf16[8,48,1280]{2,1,0:T(8,128)(2,1)S(1)} %get-tuple-element.25), channel_id=1, source_target_pairs={{0,2},{2,0},{4,6},{6,4},{8,10},{10,8},{12,14},{14,12},{16,18},{18,... | collective-permute-start | bytes 2949128 | tf_op jit(solution)/shard_map/ppermute | solution.py:272
  261.2 26.9 %collective-permute-start.29 = (bf16[16,48,1536]{2,1,0:T(8,128)(2,1)S(1)}, bf16[16,48,1536]{2,1,0:T(8,128)(2,1)S(1)}, u32[]{:S(2)}, u32[]{:S(2)}) collective-permute-start(bf16[16,48,1536]{2,1,0:T(8,128)(2,1)S(1)} %get-tuple-element.29), channel_id=1, source_target_pairs={{0,2},{2,0},{4,6},{6,4},{8,10},{10,8},{12,14},{14,12},{16,18},{18,... | collective-permute-start | bytes 7077896 | tf_op jit(solution)/shard_map/ppermute | solution.py:272
  262.5 13.4 %collective-permute-start.20 = (bf16[4,48,1280]{2,1,0:T(8,128)(2,1)S(1)}, bf16[4,48,1280]{2,1,0:T(8,128)(2,1)S(1)}, u32[]{:S(2)}, u32[]{:S(2)}) collective-permute-start(bf16[4,48,1280]{2,1,0:T(8,128)(2,1)S(1)} %get-tuple-element.90), channel_id=1, source_target_pairs={{0,4},{2,6},{4,0},{6,2},{8,12},{10,14},{12,8},{14,10},{16,20},{18,... | collective-permute-start | bytes 1474568 | tf_op jit(solution)/shard_map/ppermute | solution.py:272
  288.8 37.7 %collective-permute-start.30 = (bf16[8,48,1536]{2,1,0:T(8,128)(2,1)S(1)}, bf16[8,48,1536]{2,1,0:T(8,128)(2,1)S(1)}, u32[]{:S(2)}, u32[]{:S(2)}) collective-permute-start(bf16[8,48,1536]{2,1,0:T(8,128)(2,1)S(1)} %get-tuple-element.84), channel_id=1, source_target_pairs={{0,4},{2,6},{4,0},{6,2},{8,12},{10,14},{12,8},{14,10},{16,20},{18,... | collective-permute-start | bytes 3538952 | tf_op jit(solution)/shard_map/ppermute | solution.py:272
  292.9 35.3 %collective-permute-start.25 = (bf16[8,48,1920]{2,1,0:T(8,128)(2,1)S(1)}, bf16[8,48,1920]{2,1,0:T(8,128)(2,1)S(1)}, u32[]{:S(2)}, u32[]{:S(2)}) collective-permute-start(bf16[8,48,1920]{2,1,0:T(8,128)(2,1)S(1)} %get-tuple-element.82), channel_id=1, source_target_pairs={{0,1},{1,0},{2,3},{3,2},{4,5},{5,4},{6,7},{7,6},{8,9},{9,8},{10,11... | collective-permute-start | bytes 4423688 | tf_op jit(solution)/shard_map/ppermute | solution.py:272
  293.6 32.8 %collective-permute-start.23 = (bf16[48,512]{1,0:T(8,128)(2,1)S(1)}, bf16[48,512]{1,0:T(8,128)(2,1)S(1)}, u32[]{:S(2)}, u32[]{:S(2)}) collective-permute-start(bf16[48,512]{1,0:T(8,128)(2,1)S(1)} %fusion.30), channel_id=1, source_target_pairs={{0,1},{1,0},{2,3},{3,2},{4,5},{5,4},{6,7},{7,6},{8,9},{9,8},{10,11... | collective-permute-start | bytes 147464 | tf_op jit(solution)/shard_map/ppermute | solution.py:272
  328.6 15.5 %collective-permute-start.26 = (bf16[4,48,1920]{2,1,0:T(8,128)(2,1)S(1)}, bf16[4,48,1920]{2,1,0:T(8,128)(2,1)S(1)}, u32[]{:S(2)}, u32[]{:S(2)}) collective-permute-start(bf16[4,48,1920]{2,1,0:T(8,128)(2,1)S(1)} %get-tuple-element.86), channel_id=1, source_target_pairs={{0,4},{2,6},{4,0},{6,2},{8,12},{10,14},{12,8},{14,10},{16,20},{18,... | collective-permute-start | bytes 2211848 | tf_op jit(solution)/shard_map/ppermute | solution.py:272
  (40 other events, 618.8 us)
